TPU v7x, 32 devices: a whole 2x2x4 slice. The times are simulated.
32 devices in a mesh: row: 4 (over x, core), col: 8 (over z, y).
Axes of the slice: x: 2, y: 2, z: 4, core: 2. Of those that a mesh axis runs over, the one named last changes fastest.
Arguments:
- left_factor: bfloat16 [8, 1024, 48, 2048], P(None, 'row', None, 'col'), may hold values from -0.01953125 to 0.01953125
- prev_solution: bfloat16 [48, 2048, 512], P('row', 'col'), may hold values from -6 to 6
- cross: bfloat16 [8, 1024, 512], P(None, 'row'), may hold values from -6 to 6
- inverses: bfloat16 [2, 4, 1024, 2, 2048], P(None, None, 'row', None, 'col'), as said below
- coupling: bfloat16 [4, 1024, 2, 2048], P(None, 'row', None, 'col'), may hold values from -0.09375 to 0.09375
- prior_cov: float32 [512, 512], P('col'), may hold values from -6 to 6
Outputs:
- solved: bfloat16 [8, 1024, 512], P(None, 'row')
- pred_cov: float32 [512, 512], P('col')
Inputs may be any that keep to these rules, and one draw needn't show every extreme that they name: Each block of inverses is lower triangular in natural order, with diagonal entries from 0.5 to 1.5.
All inputs are finite; a program needn't handle non-finite values.
Results may differ from a plain program's by a relative error of at most 0.0056.
Values may be sent and summed in bfloat16 or wider, within the bound.
A program may use at most 128 MiB of HBM per device.

v0:
```python
import jax
import jax.numpy as jnp
from jax import lax
from jax.sharding import PartitionSpec as P

S = 8192


def apply_block(matrix, values):
    return jnp.einsum("atbu,bum->atm", matrix, values, preferred_element_type=jnp.float32)


def spread_rows(values):
    n_row = lax.axis_size("row")
    n_col = lax.axis_size("col")
    col_id = lax.axis_index("col")
    rounds, tile, sites = values.shape
    gathered = lax.all_gather(values, "row", axis=1, tiled=True)
    arranged = gathered.reshape(rounds * n_row // n_col, n_col * tile, sites)
    return lax.dynamic_slice_in_dim(arranged, col_id * tile, tile, 1)


def column_sum(values):
    return lax.psum(values, "col")


def solve_rounded(values):
    return lax.psum(values, "col").astype(jnp.bfloat16)


def outer_rows(solution):
    share = solution.shape[2] // lax.axis_size("col")
    own = lax.dynamic_slice_in_dim(solution, lax.axis_index("col") * share, share, 2)
    return jnp.einsum("atm,atn->mn", own, solution, preferred_element_type=jnp.float32)


def body(left_factor, prev_solution, cross, inverses, coupling, prior_cov):
    half = coupling.shape[0]
    pre = jnp.einsum(
        "atbu,bum->atm",
        left_factor,
        lax.all_gather(prev_solution, "row", axis=0, tiled=True),
        preferred_element_type=jnp.float32,
    )
    cross_first = cross[:half].astype(jnp.float32)
    cross_second = cross[half:].astype(jnp.float32)
    pre_first = lax.psum(pre[:half], "col")
    first_rhs = (cross_first - pre_first).astype(jnp.bfloat16)
    solved_first = solve_rounded(apply_block(inverses[0], spread_rows(first_rhs)))
    linked = column_sum(pre[half:] + apply_block(coupling, spread_rows(solved_first)))
    second_rhs = (cross_second - linked).astype(jnp.bfloat16)
    solved_second = solve_rounded(apply_block(inverses[1], spread_rows(second_rhs)))
    solved_all = jnp.concatenate([solved_first, solved_second], axis=0)
    outer_total = lax.psum(outer_rows(solved_all).astype(jnp.bfloat16), "row").astype(jnp.float32)
    pred_cov = prior_cov - outer_total / S
    return (solved_all, pred_cov)


def solution(mesh):
    placed = (
        P(None, "row", None, "col"),
        P("row", "col", None),
        P(None, "row", None),
        P(None, None, "row", None, "col"),
        P(None, "row", None, "col"),
        P("col", None),
    )
    return jax.shard_map(
        body,
        mesh=mesh,
        in_specs=placed,
        out_specs=(P(None, "row", None), P("col", None)),
        check_vma=False,
    )
```

profile of v0, /device:TPU:27, one launch (start us, length us, event | category | flops | bytes accessed | tf_op | source)
XLA Modules:
  0.0 706.9 jit_solution(9564156837406760404)
XLA Ops:
  7.2 0.0 copy-start
  7.2 0.0 all-gather.5.cloned.1.call-start
  7.2 0.7 all-gather.5.cloned.1.call-update
  7.9 0.0 all-reduce.6.cloned.1.call-start
  8.0 84.2 %all-gather.5.cloned.1.call-done = bf16[48,256,512]{2,1,0:T(8,128)(2,1)} async-done(((bf16[12,256,512]{2,1,0:T(8,128)(2,1)}), bf16[48,256,512]{2,1,0:T(8,128)(2,1)}) %all-gather.5.cloned.1.call-update) | async-done | bytes 12582928 | tf_op jit(solution)/shard_map/all_gather | solution.py:42
  92.2 56.9 %fusion.3 = f32[8,256,512]{2,1,0:T(8,128)} fusion(bf16[48,256,512]{2,1,0:T(8,128)(2,1)} %all-gather.5.cloned.1.call-done, bf16[8,256,48,256]{3,2,1,0:T(8,128)(2,1)} %param.6), kind=kOutput, calls=%fused_computation.6 | convolution fusion | flops 25769803776 | bytes 67108864 | tf_op jit(solution)/shard_map/atbu,bum->atm/dot_general | solution.py:39
  149.1 3.1 slice.24
  152.2 0.0 all-reduce.6.cloned.1.call-update
  152.2 0.0 copy-start.3
  152.2 0.0 all-gather.7.cloned.1.call-start
  152.3 101.3 %all-reduce.6.cloned.1.call-done = f32[4,256,512]{2,1,0:T(8,128)} async-done(((f32[4,256,512]{2,1,0:T(8,128)}), f32[4,256,512]{2,1,0:T(8,128)}) %all-reduce.6.cloned.1.call-update) | async-done | bytes 2097168 | tf_op jit(solution)/shard_map/psum | solution.py:47
  253.6 3.2 subtract_convert_fusion.1
  256.7 0.0 all-gather.7.cloned.1.call-update
  256.7 0.0 all-gather.9.cloned.1.call-start
  256.8 0.0 copy-done.3
  256.8 2.5 fusion.23
  259.3 32.5 %all-gather.7.cloned.1.call-done = bf16[4,1024,512]{2,1,0:T(8,128)(2,1)} async-done(((bf16[4,256,512]{2,1,0:T(8,128)(2,1)}), bf16[4,1024,512]{2,1,0:T(8,128)(2,1)}) %all-gather.7.cloned.1.call-update) | async-done | bytes 4194320 | tf_op jit(solution)/shard_map/all_gather | solution.py:18
  291.8 2.1 convolution_bitcast_fusion.1
  293.9 82.6 %all-reduce.11 = bf16[4,256,512]{1,2,0:T(8,128)(2,1)} all-reduce(f32[4,256,512]{1,2,0:T(8,128)S(1)} %convolution_bitcast_fusion.1), channel_id=1, replica_groups=mesh['row'=4,'col'=8] {'col'}, use_global_device_ids=true, to_apply=%region_1.0 | all-reduce | flops 524288 | bytes 3145728 | tf_op jit(solution)/shard_map/psum | solution.py:28
  376.5 0.0 all-gather.9.cloned.1.call-update
  376.5 0.0 all-reduce.8.cloned.1.call-start
  376.6 44.7 %all-gather.9.cloned.1.call-done = bf16[4,1024,512]{1,2,0:T(8,128)(2,1)} async-done(((bf16[4,256,512]{1,2,0:T(8,128)(2,1)}), bf16[4,1024,512]{1,2,0:T(8,128)(2,1)}) %all-gather.9.cloned.1.call-update) | async-done | bytes 4194320 | tf_op jit(solution)/shard_map/all_gather | solution.py:18
  421.3 6.3 copy.31
  427.6 0.0 copy-done
  427.6 3.8 slice_add_fusion
  431.4 0.0 all-reduce.8.cloned.1.call-update
  431.4 0.0 copy-start.2
  431.4 0.0 all-gather.11.cloned.1.call-start
  431.5 101.3 %all-reduce.8.cloned.1.call-done = f32[4,256,512]{2,1,0:T(8,128)} async-done(((f32[4,256,512]{2,1,0:T(8,128)}), f32[4,256,512]{2,1,0:T(8,128)}) %all-reduce.8.cloned.1.call-update) | async-done | bytes 2097168 | tf_op jit(solution)/shard_map/psum | solution.py:24
  532.8 3.2 subtract_convert_fusion
  536.0 0.0 all-gather.11.cloned.1.call-update
  536.0 0.0 all-reduce.10.cloned.1.call-start
  536.0 35.0 %all-gather.11.cloned.1.call-done = bf16[4,1024,512]{2,1,0:T(8,128)(2,1)} async-done(((bf16[4,256,512]{2,1,0:T(8,128)(2,1)}), bf16[4,1024,512]{2,1,0:T(8,128)(2,1)}) %all-gather.11.cloned.1.call-update) | async-done | bytes 4194320 | tf_op jit(solution)/shard_map/all_gather | solution.py:18
  571.0 0.0 copy-done.2
  571.0 3.1 convolution_bitcast_fusion
  574.1 0.0 copy-start.1
  574.1 83.1 %all-reduce.12 = bf16[4,256,512]{1,2,0:T(8,128)(2,1)S(1)} all-reduce(f32[4,256,512]{1,2,0:T(8,128)} %convolution_bitcast_fusion), channel_id=1, replica_groups=mesh['row'=4,'col'=8] {'col'}, use_global_device_ids=true, to_apply=%region_3.0 | all-reduce | flops 524288 | bytes 3145728 | tf_op jit(solution)/shard_map/psum | solution.py:28
  657.3 0.0 copy-done.1
  657.3 1.4 fusion.8
  658.7 0.0 all-reduce.10.cloned.1.call-update
  658.7 1.5 pad_maximum_fusion
  660.2 0.0 copy-start.4
  660.2 4.0 copy.38
  664.2 34.3 %all-reduce.10.cloned.1.call-done = bf16[64,512]{1,0:T(8,128)(2,1)} async-done(((bf16[64,512]{1,0:T(8,128)(2,1)}), bf16[64,512]{1,0:T(8,128)(2,1)}) %all-reduce.10.cloned.1.call-update) | async-done | bytes 65552 | tf_op jit(solution)/shard_map/psum | solution.py:54
  698.5 0.0 copy-done.4
  698.5 1.5 multiply_subtract_fusion
Async XLA Ops:
  7.2 420.4 %copy-start = (bf16[4,256,2,256]{3,2,1,0:T(2,128)(2,1)S(1)}, bf16[4,256,2,256]{3,2,1,0:T(2,128)(2,1)}, u32[]{:S(2)}) copy-start(bf16[4,256,2,256]{3,2,1,0:T(2,128)(2,1)} %param.10) | copy-start | bytes 3145732
  7.2 85.0 %all-gather.5.cloned.1.call-start = ((), (), s32[]{:S(2)}) async-start(), calls=%async_computation | async-start | bytes 15728640 | tf_op jit(solution)/shard_map/all_gather | solution.py:42
  7.9 245.6 %all-reduce.6.cloned.1.call-start = ((), (), s32[]{:S(2)}) async-start(), calls=%async_computation.1 | async-start | bytes 4194304 | tf_op jit(solution)/shard_map/psum | solution.py:47
  152.2 104.6 %copy-start.3 = (bf16[2,4,256,2,256]{4,3,2,1,0:T(2,128)(2,1)S(1)}, bf16[2,4,256,2,256]{4,3,2,1,0:T(2,128)(2,1)}, u32[]{:S(2)}) copy-start(bf16[2,4,256,2,256]{4,3,2,1,0:T(2,128)(2,1)} %param.9) | copy-start | bytes 6291460
  152.2 139.5 %all-gather.7.cloned.1.call-start = ((), (), s32[]{:S(2)}) async-start(), calls=%async_computation.2 | async-start | bytes 5242880 | tf_op jit(solution)/shard_map/all_gather | solution.py:18
  256.7 164.6 %all-gather.9.cloned.1.call-start = ((), (), s32[]{:S(2)}) async-start(), calls=%async_computation.3 | async-start | bytes 5242880 | tf_op jit(solution)/shard_map/all_gather | solution.py:18
  376.5 156.3 %all-reduce.8.cloned.1.call-start = ((), (), s32[]{:S(2)}) async-start(), calls=%async_computation.4 | async-start | bytes 4194304 | tf_op jit(solution)/shard_map/psum | solution.py:24
  431.4 139.6 %copy-start.2 = (bf16[1,4,256,2,256]{4,3,2,1,0:T(2,128)(2,1)S(1)}, bf16[1,4,256,2,256]{4,3,2,1,0:T(2,128)(2,1)}, u32[]{:S(2)}) copy-start(bf16[1,4,256,2,256]{4,3,2,1,0:T(2,128)(2,1)} %get-tuple-element.9) | copy-start | bytes 3145732
  431.4 139.6 %all-gather.11.cloned.1.call-start = ((), (), s32[]{:S(2)}) async-start(), calls=%async_computation.5 | async-start | bytes 5242880 | tf_op jit(solution)/shard_map/all_gather | solution.py:18
  536.0 162.5 %all-reduce.10.cloned.1.call-start = ((), (), s32[]{:S(2)}) async-start(), calls=%async_computation.6 | async-start | bytes 131072 | tf_op jit(solution)/shard_map/psum | solution.py:54
  574.1 83.2 %copy-start.1 = (bf16[4,256,512]{1,2,0:T(8,128)(2,1)S(1)}, bf16[4,256,512]{1,2,0:T(8,128)(2,1)}, u32[]{:S(2)}) copy-start(bf16[4,256,512]{1,2,0:T(8,128)(2,1)} %all-reduce.11) | copy-start | bytes 3145732
  660.2 38.3 %copy-start.4 = (f32[64,512]{1,0:T(8,128)S(1)}, f32[64,512]{1,0:T(8,128)}, u32[]{:S(2)}) copy-start(f32[64,512]{1,0:T(8,128)} %param.11) | copy-start | bytes 393220
Sparse Core Ops, SparseCore 0:
  9.6 82.5 all-gather.4
  152.3 101.1 all-reduce.5
  256.9 34.8 all-gather.6
  376.6 44.6 all-gather.8
  431.5 101.2 all-reduce.7
  536.1 34.8 all-gather.10
  658.8 39.6 all-reduce.9
where the time goes:
time: 711 us; the launch traced here: 707 us
  waiting for transfers between devices  434 us (61%)
  blocking collectives  166 us (23%)
  matrix products  67.4 us (9%)
  local copies, waits for them, and re-layouts  15.8 us (2%)
  between operations  14.2 us (2%)
  other arithmetic  9.36 us (1%)
    psum x2, blocking collectives, solve_rounded(): return lax.psum(values, 'col').astype(jnp.bfloat16)  166 us
    all_gather x3, waiting for transfers between devices, spread_rows(): gathered = lax.all_gather(values, 'row', axis=1, tiled=True)  112 us
    psum x1, waiting for transfers between devices, column_sum(): return lax.psum(values, 'col')  101 us
    psum x1, waiting for transfers between devices, body(): pre_first = lax.psum(pre[:half], 'col')  101 us
    all_gather x1, waiting for transfers between devices, body(): lax.all_gather(prev_solution, 'row', axis=0, tiled=True)  84.2 us
    dot_general x1, matrix products, body(): jnp.einsum('atbu,bum->atm', left_factor, lax.all_gather(prev_solution, 'r...  56.9 us
    psum x1, waiting for transfers between devices, body(): lax.psum(outer_rows(solved_all).astype(jnp.bfloat16), 'row')  34.3 us
  transfers between devices with their start and end apart: 7, of which 7 were waited for; matrix products, arithmetic and copies ran while one was open for 1% of the time, Pallas kernels for 0%

commit v1 on v0

v1 whole, which is shorter than its diff:
```python
import functools

import jax
import jax.numpy as jnp
from jax import lax
from jax.experimental import pallas as pl
from jax.experimental.pallas import tpu as pltpu
from jax.sharding import PartitionSpec as P

F32, BF16 = jnp.float32, jnp.bfloat16
PIECES = 2
MESH = pl.DeviceIdType.MESH


def chain_kernel(
    n_row, n_col, total_rows,
    pre_ref, cross_ref, gown_ref, gpair_ref, prior_ref,
    out_ref, cov_ref,
    part, second, stage, land, rhs, sol, pair_out, pair_in, cov_out, cov_in, cov_all,
    s_pair, r_pair, s_red, r_red, s_x, r_x, s_core, r_core,
    s_gat, r_gat, s_fwd, r_fwd, s_cov, r_cov,
):
    tiles, tile, sites = pre_ref.shape
    half = tiles // 2
    n_z = n_col // 2
    owners = n_col // n_row
    per = half // owners
    mh = sites // 2
    width = mh // PIECES
    band = n_row // 2

    row, col = lax.axis_index("row"), lax.axis_index("col")
    z, y = col // 2, col % 2
    core = row % 2
    mate_col = col + 1 - 2 * y
    mate_row = row + 1 - 2 * core
    mine = z // band
    active = z % band == row // 2

    def remote(src, dst, send, recv, r, c):
        return pltpu.make_async_remote_copy(
            src_ref=src, dst_ref=dst, send_sem=send, recv_sem=recv,
            device_id={"row": r, "col": c}, device_id_type=MESH)

    barrier = pltpu.get_barrier_semaphore()
    count = 1
    pl.semaphore_signal(barrier, inc=1, device_id={"row": row, "col": mate_col}, device_id_type=MESH)
    for dr in range(n_row):
        for dz in range(n_z):
            if dr or dz:
                count += 1
                pl.semaphore_signal(
                    barrier, inc=1,
                    device_id={"row": (row + dr) % n_row, "col": ((z + dz) % n_z) * 2 + y},
                    device_id_type=MESH)
    pl.semaphore_wait(barrier, count)

    def lanes(h, p):
        return pl.ds(pl.multiple_of(h * mh + p * width, 128), width)

    def pair_copy(panel, p):
        return remote(pair_out.at[panel, p], pair_in.at[panel, p], s_pair.at[panel, p], r_pair.at[panel, p], row, mate_col)

    for panel in range(2):
        for p in range(PIECES):
            for a in range(half):
                pair_out[panel, p, a] = pre_ref[panel * half + a, :, lanes(1 - y, p)].astype(BF16)
            pair_copy(panel, p).start()

    def pair_sum(panel, p, a):
        return pre_ref[panel * half + a, :, lanes(y, p)] + pair_in[panel, p, a].astype(F32)

    def reduce_copy(f, p, i):
        owner_z = i * band + row // 2
        slot = (z - owner_z + n_z) % n_z - 1
        return remote(stage.at[f, p, i], land.at[f, p, slot], s_red.at[f, p, i], r_red.at[f, p, slot], row, owner_z * 2 + y)

    def not_owner(i):
        return z != i * band + row // 2

    def send_parts(f, p):
        for i in range(owners):
            for k in range(per):
                stage[f, p, i, k] = part[p, i + owners * k].astype(BF16)

            @pl.when(not_owner(i))
            def _():
                reduce_copy(f, p, i).start()

    def wait_landed(f, p, slot):
        remote(land.at[f, p, slot], land.at[f, p, slot], s_red.at[f, p, 0], r_red.at[f, p, slot], row, mate_col).wait_recv()

    def x_copy(f, p, j):
        peer = (row + 2 * j) % n_row
        return remote(rhs.at[f, p, core], rhs.at[f, p, core], s_x.at[f, p, j - 1], r_x.at[f, p], peer, col)

    def core_copy(f, p):
        return remote(rhs.at[f, p, core], rhs.at[f, p, core], s_core.at[f, p], r_core.at[f, p], mate_row, col)

    def core_wait(f, p):
        remote(rhs.at[f, p, 1 - core], rhs.at[f, p, 1 - core], s_core.at[f, p], r_core.at[f, p], mate_row, col).wait_recv()

    def gather_copy(g, p, dz):
        return remote(sol.at[y, g, p, mine], sol.at[y, g, p, mine], s_gat.at[g, p, dz - 1], r_gat.at[g, p, mine], row, ((z + dz) % n_z) * 2 + y)

    def forward_copy(g, p, i):
        return remote(sol.at[y, g, p, i], sol.at[y, g, p, i], s_fwd.at[g, p, i], r_fwd.at[g, p, i], row, mate_col)

    def take(f, p):
        @pl.when(active)
        def _():
            for slot in range(n_z - 1):
                wait_landed(f, p, slot)
            for k in range(per):
                total = part[p, mine + owners * k]
                for slot in range(n_z - 1):
                    total = total + land[f, p, slot, k].astype(F32)
                if f % 2 == 0:
                    total = cross_ref[(f // 2) * half + mine + owners * k, :, lanes(y, p)].astype(F32) - total
                value = total.astype(BF16)
                if f < 3:
                    rhs[f, p, core, k] = value
                if f % 2 == 1:
                    sol[y, f // 2, p, mine, k] = value
            if f < 3:
                for j in range(1, band):
                    x_copy(f, p, j).start()
            if f % 2 == 1:
                for dz in range(1, n_z):
                    gather_copy(f // 2, p, dz).start()

        if f < 3:
            @pl.when(jnp.logical_not(active))
            def _():
                remote(rhs.at[f, p, core], rhs.at[f, p, core], s_core.at[f, p], r_x.at[f, p], mate_row, col).wait_recv()
            core_copy(f, p).start()
            core_wait(f, p)

    def apply(f, p):
        near = rhs[f - 1, p, y].reshape(per * tile, width)
        far = rhs[f - 1, p, 1 - y].reshape(per * tile, width)
        for a in range(half):
            rows = pl.ds(a * tile, tile)
            got = jnp.dot(gown_ref[f - 1, rows, :], near, preferred_element_type=F32)
            got = got + jnp.dot(gpair_ref[f - 1, rows, :], far, preferred_element_type=F32)
            if f == 2:
                got = got + second[p, a]
            part[p, a] = got

    def gather_on(g, p):
        for i in range(owners):
            @pl.when(not_owner(i))
            def _():
                remote(sol.at[y, g, p, i], sol.at[y, g, p, i], s_fwd.at[g, p, i], r_gat.at[g, p, i], row, mate_col).wait_recv()
            forward_copy(g, p, i).start()

    def gather_end(g, p):
        for i in range(owners):
            remote(sol.at[1 - y, g, p, i], sol.at[1 - y, g, p, i], s_fwd.at[g, p, i], r_fwd.at[g, p, i], row, mate_col).wait_recv()
        for h in range(2):
            for i in range(owners):
                for k in range(per):
                    out_ref[g * half + i + owners * k, :, pl.ds(h * mh + p * width, width)] = sol[h, g, p, i, k]

    share = prior_ref.shape[0]
    block = pl.multiple_of(col * share // 128 * 128, 128)

    def outer(g):
        rows = half * tile
        own = out_ref[pl.ds(g * half, half), :, pl.ds(block, 128)].reshape(rows, 128)
        every = out_ref[pl.ds(g * half, half)].reshape(rows, sites)
        return lax.dot_general(own, every, (((0,), (0,)), ((), ())), preferred_element_type=F32)

    for p in range(PIECES):
        pair_copy(0, p).wait_recv()
        for a in range(half):
            part[p, a] = pair_sum(0, p, a)
        send_parts(0, p)
    for p in range(PIECES):
        pair_copy(1, p).wait_recv()
        for a in range(half):
            second[p, a] = pair_sum(1, p, a)
    for f in range(4):
        for p in range(PIECES):
            take(f, p)
            if f < 3:
                apply(f + 1, p)
                send_parts(f + 1, p)
            if f == 2:
                gather_on(0, p)
    for p in range(PIECES):
        gather_end(0, p)
    cov_all[...] = outer(0)
    for p in range(PIECES):
        gather_on(1, p)
    for p in range(PIECES):
        gather_end(1, p)
    cov_all[...] += outer(1)

    rows = pl.ds(pl.multiple_of(col * share % 128, share), share)
    own_cov = cov_all[rows, :]
    cov_out[...] = own_cov.astype(BF16)

    def cov_copy(j):
        return remote(cov_out, cov_in.at[j - 1], s_cov.at[j - 1], r_cov.at[j - 1], (row + j) % n_row, col)

    for j in range(1, n_row):
        cov_copy(j).start()
    total = own_cov
    for j in range(1, n_row):
        cov_copy(j).wait_recv()
        total = total + cov_in[j - 1].astype(F32)
    cov_ref[...] = prior_ref[...] - total / total_rows

    for j in range(1, n_row):
        cov_copy(j).wait_send()
    for p in range(PIECES):
        for panel in range(2):
            pair_copy(panel, p).wait_send()
            for i in range(owners):
                forward_copy(panel, p, i).wait_send()
        for f in range(4):
            for i in range(owners):
                @pl.when(not_owner(i))
                def _():
                    reduce_copy(f, p, i).wait_send()
            if f < 3:
                core_copy(f, p).wait_send()

        @pl.when(active)
        def _():
            for f in range(3):
                for j in range(1, band):
                    x_copy(f, p, j).wait_send()
            for g in range(2):
                for dz in range(1, n_z):
                    gather_copy(g, p, dz).wait_send()


def chain(n_row, n_col, pre, cross, gown, gpair, prior):
    tiles, tile, sites = pre.shape
    half, n_z, owners, band = tiles // 2, n_col // 2, n_col // n_row, n_row // 2
    per = half // owners
    width = sites // 2 // PIECES
    share = prior.shape[0]
    dma = pltpu.SemaphoreType.DMA
    vm = pl.BlockSpec(memory_space=pltpu.VMEM)
    return pl.pallas_call(
        functools.partial(chain_kernel, n_row, n_col, tiles * tile * n_row),
        out_shape=(
            jax.ShapeDtypeStruct((tiles, tile, sites), BF16),
            jax.ShapeDtypeStruct((share, sites), F32),
        ),
        in_specs=[vm] * 5,
        out_specs=(vm, vm),
        scratch_shapes=[
            pltpu.VMEM((PIECES, half, tile, width), F32),
            pltpu.VMEM((PIECES, half, tile, width), F32),
            pltpu.VMEM((4, PIECES, owners, per, tile, width), BF16),
            pltpu.VMEM((4, PIECES, n_z - 1, per, tile, width), BF16),
            pltpu.VMEM((3, PIECES, 2, per, tile, width), BF16),
            pltpu.VMEM((2, 2, PIECES, owners, per, tile, width), BF16),
            pltpu.VMEM((2, PIECES, half, tile, width), BF16),
            pltpu.VMEM((2, PIECES, half, tile, width), BF16),
            pltpu.VMEM((share, sites), BF16),
            pltpu.VMEM((n_row - 1, share, sites), BF16),
            pltpu.VMEM((128, sites), F32),
            dma((2, PIECES)), dma((2, PIECES)),
            dma((4, PIECES, owners)), dma((4, PIECES, n_z - 1)),
            dma((3, PIECES, max(band - 1, 1))), dma((3, PIECES)),
            dma((3, PIECES)), dma((3, PIECES)),
            dma((2, PIECES, n_z - 1)), dma((2, PIECES, owners)),
            dma((2, PIECES, owners)), dma((2, PIECES, owners)),
            dma((n_row - 1,)), dma((n_row - 1,)),
        ],
        compiler_params=pltpu.CompilerParams(
            collective_id=0, has_side_effects=True, vmem_limit_bytes=48 * 1024 * 1024),
    )(pre, cross, gown, gpair, prior)


def body(n_row, n_col, left_factor, prev_solution, cross, inverses, coupling, prior_cov):
    half, tile, cols, _ = coupling.shape
    blocks = jnp.stack([inverses[0], coupling, inverses[1]]).reshape(3, half * tile, cols * tile)
    mate = lax.ppermute(blocks, "col", [(c, c ^ 1) for c in range(n_col)])
    pre = jnp.einsum(
        "atbu,bum->atm",
        left_factor,
        lax.all_gather(prev_solution, "row", axis=0, tiled=True),
        preferred_element_type=F32,
    )
    return chain(n_row, n_col, pre, cross, blocks, mate, prior_cov)


def solution(mesh):
    placed = (
        P(None, "row", None, "col"),
        P("row", "col", None),
        P(None, "row", None),
        P(None, None, "row", None, "col"),
        P(None, "row", None, "col"),
        P("col", None),
    )
    return jax.shard_map(
        functools.partial(body, mesh.shape["row"], mesh.shape["col"]),
        mesh=mesh,
        in_specs=placed,
        out_specs=(P(None, "row", None), P("col", None)),
        check_vma=False,
    )
```

time: 711 us -> 276 us (0.39)
  waiting for transfers between devices: 434 us -> 73.5 us
  blocking collectives: 166 us -> 0 us
  Pallas kernels: 0 us -> 118 us
  matrix products: 67.4 us -> 56.9 us
  other arithmetic: 9.36 us -> 0 us
    psum x3 -> x0, waiting for transfers between devices: 237 us -> none  [the longest x1 101 us: column_sum(): return lax.psum(values, 'col')]
    psum x2 -> x0, blocking collectives: 166 us -> none  [solve_rounded(): return lax.psum(values, 'col').astype(jnp.bfloat16)]
    pallas_call x0 -> x1, Pallas kernels: none -> 118 us  [chain(): pl.pallas_call(functools.partial(chain_kernel, n_row, n_col, tiles * tile...]
    all_gather x3 -> x0, waiting for transfers between devices: 112 us -> none  [spread_rows(): gathered = lax.all_gather(values, 'row', axis=1, tiled=True)]
    all_gather x1, waiting for transfers between devices: 84.2 us -> 72.8 us  [body(): lax.all_gather(prev_solution, 'row', axis=0, tiled=True)]
    dot_general x4 -> x0, matrix products: 10.5 us -> none  [the longest x3 9.07 us: apply_block(): jnp.einsum('atbu,bum->atm', matrix, values, preferred_element_type=jnp.fl...]
  transfers between devices with their start and end apart: 7 -> 2, of which waited for: 7 -> 1; matrix products, arithmetic and copies ran while one was open for 1% -> 24% of each run, Pallas kernels for 0% -> 0%
where the time goes in v1:
time: 276 us
  Pallas kernels  118 us (43%)
  waiting for transfers between devices  73.5 us (27%)
  matrix products  56.9 us (21%)
  between operations  14.1 us (5%)
  local copies, waits for them, and re-layouts  12.2 us (4%)
    pallas_call x1, Pallas kernels, chain(): pl.pallas_call(functools.partial(chain_kernel, n_row, n_col, tiles * tile...  118 us
    all_gather x1, waiting for transfers between devices, body(): lax.all_gather(prev_solution, 'row', axis=0, tiled=True)  72.8 us
    dot_general x1, matrix products, body(): jnp.einsum('atbu,bum->atm', left_factor, lax.all_gather(prev_solution, 'r...  56.9 us
  transfers between devices with their start and end apart: 2, of which 1 were waited for; matrix products, arithmetic and copies ran while one was open for 24% of the time, Pallas kernels for 0%

profile of v1, /device:TPU:27, one launch (start us, length us, event | category | flops | bytes accessed | tf_op | source)
XLA Modules:
  0.0 276.3 jit_solution(8491884743458850232)
XLA Ops:
  7.2 0.0 copy-start.2
  7.2 0.0 all-gather.2.cloned.1.call-start
  7.2 0.7 all-gather.2.cloned.1.call-update
  7.9 0.5 copy-done.2
  8.4 0.7 stack.11
  9.1 3.5 %fusion.8 = (bf16[1,4,256,2,256]{4,3,2,1,0:T(2,128)(2,1)S(1)}, bf16[1,4,256,2,256]{4,3,2,1,0:T(2,128)(2,1)}) fusion(bf16[2,4,256,2,256]{4,3,2,1,0:T(2,128)(2,1)} %param.9), kind=kLoop, calls=%fused_computation.7 | loop fusion | bytes 4194304 | tf_op jit(solution)/shard_map/slice | solution.py:283
  12.5 0.7 stack.12
  13.2 1.7 stack.10
  15.0 1.1 constant_dynamic-update-slice_fusion.2
  16.0 1.0 constant_dynamic-update-slice_fusion.1
  17.1 1.1 constant_dynamic-update-slice_fusion.gown_ref
  18.1 0.0 copy-start
  18.1 0.0 copy-start.1
  18.1 1.2 collective-permute-start
  19.4 72.8 %all-gather.2.cloned.1.call-done = bf16[48,256,512]{2,1,0:T(8,128)(2,1)} async-done(((bf16[12,256,512]{2,1,0:T(8,128)(2,1)}), bf16[48,256,512]{2,1,0:T(8,128)(2,1)}) %all-gather.2.cloned.1.call-update) | async-done | bytes 12582928 | tf_op jit(solution)/shard_map/all_gather | solution.py:288
  92.2 56.9 %fusion.3.pre_ref = f32[8,256,512]{2,1,0:T(8,128)} fusion(bf16[48,256,512]{2,1,0:T(8,128)(2,1)} %all-gather.2.cloned.1.call-done, bf16[8,256,48,256]{3,2,1,0:T(8,128)(2,1)} %param.6), kind=kOutput, calls=%fused_computation.3 | convolution fusion | flops 25769803776 | bytes 67108864 | tf_op jit(solution)/shard_map/atbu,bum->atm/dot_general | solution.py:285
  149.1 0.0 collective-permute-done.gpair_ref
  149.1 0.0 copy-done
  149.1 0.0 copy-done.1
  149.1 118.3 %shard_map.77 = (bf16[8,256,512]{2,1,0:T(8,128)(2,1)S(1)}, f32[64,512]{1,0:T(8,128)S(1)}) custom-call(f32[8,256,512]{2,1,0:T(8,128)} %fusion.3.pre_ref, bf16[8,256,512]{2,1,0:T(8,128)(2,1)S(1)} %copy-done, bf16[3,1024,512]{2,1,0:T(8,128)(2,1)} %constant_dynamic-update-slice_fusion.gown_ref, bf16[3,1024,512]{2,1,0:T(8,128)(2,1)} %collective-permute-done.gpair_ref, ...), custom_call_target="tpu_custom_call" | custom-call | tf_op jit(solution)/shard_map/pallas_call | solution.py:248
  267.4 1.3 copy.19
  268.8 0.7 copy.20
Async XLA Ops:
  7.2 1.2 copy-start.2
  7.2 85.0 %all-gather.2.cloned.1.call-start = ((), (), s32[]{:S(2)}) async-start(), calls=%async_computation | async-start | bytes 15728640 | tf_op jit(solution)/shard_map/all_gather | solution.py:288
  18.1 130.9 %copy-start = (bf16[8,256,512]{2,1,0:T(8,128)(2,1)S(1)}, bf16[8,256,512]{2,1,0:T(8,128)(2,1)}, u32[]{:S(2)}) copy-start(bf16[8,256,512]{2,1,0:T(8,128)(2,1)} %cross_ref.1) | copy-start | bytes 6291460
  18.1 130.9 %copy-start.1 = (f32[64,512]{1,0:T(8,128)S(1)}, f32[64,512]{1,0:T(8,128)}, u32[]{:S(2)}) copy-start(f32[64,512]{1,0:T(8,128)} %prior_ref.1) | copy-start | bytes 393220
  18.1 130.9 %collective-permute-start = (bf16[3,1024,512]{2,1,0:T(8,128)(2,1)}, bf16[3,1024,512]{2,1,0:T(8,128)(2,1)}, u32[]{:S(2)}, u32[]{:S(2)}) collective-permute-start(bf16[3,1024,512]{2,1,0:T(8,128)(2,1)} %constant_dynamic-update-slice_fusion.gown_ref), channel_id=1, source_target_pairs={{0,1},{1,0},{2,3},{3,2},{4,5},{5,4},{6,7},{7,6},{8,9},{9,8},{10,11... | collective-permute-start | bytes 9437192 | tf_op jit(solution)/shard_map/ppermute | solution.py:284
Sparse Core Ops, SparseCore 0:
  9.6 82.5 all-gather.1

commit v2 on v1

--- a/solution.py
+++ b/solution.py
@@ -13,12 +13,13 @@
 
 
 def chain_kernel(
-    n_row, n_col, total_rows,
-    pre_ref, cross_ref, gown_ref, gpair_ref, prior_ref,
+    n_row, n_col, chunk, local, total_rows,
+    left_ref, prev_ref, cross_ref, ginv_ref, gmid_ref, prior_ref,
     out_ref, cov_ref,
-    part, second, stage, land, rhs, sol, pair_out, pair_in, cov_out, cov_in, cov_all,
+    pre_ref, solved_rows, left_buf, pinv, pmid, part, stage, land, rhs, sol, pair_out, pair_in, cov_out, cov_in, cov_all,
     s_pair, r_pair, s_red, r_red, s_x, r_x, s_core, r_core,
     s_gat, r_gat, s_fwd, r_fwd, s_cov, r_cov,
+    l_own, l_left, s_vx, r_vx, s_vc, r_vc, s_g, r_g,
 ):
     tiles, tile, sites = pre_ref.shape
     half = tiles // 2
@@ -41,6 +42,18 @@
         return pltpu.make_async_remote_copy(
             src_ref=src, dst_ref=dst, send_sem=send, recv_sem=recv,
             device_id={"row": r, "col": c}, device_id_type=MESH)
+
+    held = prev_ref.shape[0]
+    rounds = left_ref.shape[2]
+    wide = 2 * width
+
+    def own_copy(p):
+        return pltpu.make_async_copy(
+            prev_ref.at[:, :, pl.ds(p * wide, wide)],
+            solved_rows.at[p, pl.ds(row * held, held)], l_own.at[p])
+
+    for p in range(PIECES):
+        own_copy(p).start()
 
     barrier = pltpu.get_barrier_semaphore()
     count = 1
@@ -56,13 +69,13 @@
     pl.semaphore_wait(barrier, count)
 
     def lanes(h, p):
-        return pl.ds(pl.multiple_of(h * mh + p * width, 128), width)
+        return pl.ds(pl.multiple_of(p * wide + h * width, 128), width)
 
     def pair_copy(panel, p):
         return remote(pair_out.at[panel, p], pair_in.at[panel, p], s_pair.at[panel, p], r_pair.at[panel, p], row, mate_col)
 
-    for panel in range(2):
-        for p in range(PIECES):
+    def pair_start(p):
+        for panel in range(2):
             for a in range(half):
                 pair_out[panel, p, a] = pre_ref[panel * half + a, :, lanes(1 - y, p)].astype(BF16)
             pair_copy(panel, p).start()
@@ -139,12 +152,18 @@
     def apply(f, p):
         near = rhs[f - 1, p, y].reshape(per * tile, width)
         far = rhs[f - 1, p, 1 - y].reshape(per * tile, width)
+        if f == 2:
+            pair_copy(1, p).wait_recv()
+        if p == 0:
+            block_copy(f - 1).wait_recv()
         for a in range(half):
             rows = pl.ds(a * tile, tile)
-            got = jnp.dot(gown_ref[f - 1, rows, :], near, preferred_element_type=F32)
-            got = got + jnp.dot(gpair_ref[f - 1, rows, :], far, preferred_element_type=F32)
+            here = gmid_ref[rows, :] if f == 2 else ginv_ref[f // 2, rows, :]
+            there = pmid[rows, :] if f == 2 else pinv[f // 2, rows, :]
+            got = jnp.dot(here, near, preferred_element_type=F32)
+            got = got + jnp.dot(there, far, preferred_element_type=F32)
             if f == 2:
-                got = got + second[p, a]
+                got = got + pair_sum(1, p, a)
             part[p, a] = got
 
     def gather_on(g, p):
@@ -160,7 +179,7 @@
         for h in range(2):
             for i in range(owners):
                 for k in range(per):
-                    out_ref[g * half + i + owners * k, :, pl.ds(h * mh + p * width, width)] = sol[h, g, p, i, k]
+                    out_ref[g * half + i + owners * k, :, pl.ds(p * wide + h * width, width)] = sol[h, g, p, i, k]
 
     share = prior_ref.shape[0]
     block = pl.multiple_of(col * share // 128 * 128, 128)
@@ -171,30 +190,128 @@
         every = out_ref[pl.ds(g * half, half)].reshape(rows, sites)
         return lax.dot_general(own, every, (((0,), (0,)), ((), ())), preferred_element_type=F32)
 
-    for p in range(PIECES):
+    def rows_of(p, r):
+        return solved_rows.at[p, pl.ds(r * held, held)]
+
+    def cross_copy(p, j):
+        return remote(rows_of(p, row), rows_of(p, row), s_vx.at[p, j - 1], r_vx.at[p, j - 1], (row + 2 * j) % n_row, col)
+
+    def cross_wait(p, j):
+        src = rows_of(p, (row + n_row - 2 * j) % n_row)
+        remote(src, src, s_vx.at[p, j - 1], r_vx.at[p, j - 1], mate_row, col).wait_recv()
+
+    def hand_copy(p, j):
+        src = rows_of(p, (row + n_row - 2 * j) % n_row)
+        return remote(src, src, s_vc.at[p, j], r_vc.at[p, j], mate_row, col)
+
+    def hand_wait(p, j):
+        src = rows_of(p, (mate_row + n_row - 2 * j) % n_row)
+        remote(src, src, s_vc.at[p, j], r_vc.at[p, j], mate_row, col).wait_recv()
+
+    def block_copy(n):
+        src = gmid_ref if n == 1 else ginv_ref.at[n // 2]
+        dst = pmid if n == 1 else pinv.at[n // 2]
+        return remote(src, dst, s_g.at[n], r_g.at[n], row, mate_col)
+
+    def product(first, chunks, pieces, fresh):
+        steps = tiles * chunks
+
+        def fetch(s, slot):
+            at = pl.multiple_of((first + s % chunks) * chunk, chunk)
+            return pltpu.make_async_copy(left_ref.at[s // chunks, :, pl.ds(at, chunk), :], left_buf.at[slot], l_left.at[slot])
+
+        fetch(0, 0).start()
+
+        def step(s, carry):
+            slot = s % 2
+
+            @pl.when(s + 1 < steps)
+            def _():
+                fetch(s + 1, 1 - slot).start()
+
+            fetch(s, slot).wait()
+            at = (first + s % chunks) * chunk
+            block = left_buf[slot].reshape(tile, chunk * tile)
+            for p in pieces:
+                values = solved_rows[p, pl.ds(at, chunk)].reshape(chunk * tile, wide)
+                got = jnp.dot(block, values, preferred_element_type=F32)
+                where = (s // chunks, slice(None), pl.ds(p * wide, wide))
+                if fresh:
+                    pre_ref[where] = got
+                else:
+                    pre_ref[where] += got
+            return carry
+
+        lax.fori_loop(0, steps, step, 0)
+
+    def bring(p):
+        for j in range(1, band):
+            cross_wait(p, j)
+            hand_copy(p, j).start()
+        if p + 1 < PIECES:
+            for j in range(1, band):
+                cross_copy(p, j).wait_send()
+            for j in range(1, band):
+                cross_copy(p + 1, j).start()
+        for j in range(1, band):
+            hand_wait(p, j)
+
+    def rest(p):
+        if local:
+            product((1 - row // 2), rounds // chunk - 1, (p,), False)
+        else:
+            for n in range(rounds // chunk):
+                product(n, 1, (p,), n == 0)
+
+    def first_sum(p):
         pair_copy(0, p).wait_recv()
         for a in range(half):
             part[p, a] = pair_sum(0, p, a)
         send_parts(0, p)
+
+    def advance(f, p):
+        take(f, p)
+        if f < 3:
+            apply(f + 1, p)
+            send_parts(f + 1, p)
+
     for p in range(PIECES):
-        pair_copy(1, p).wait_recv()
-        for a in range(half):
-            second[p, a] = pair_sum(1, p, a)
-    for f in range(4):
-        for p in range(PIECES):
-            take(f, p)
-            if f < 3:
-                apply(f + 1, p)
-                send_parts(f + 1, p)
-            if f == 2:
-                gather_on(0, p)
+        own_copy(p).wait()
+        hand_copy(p, 0).start()
+        if p == 0:
+            for j in range(1, band):
+                cross_copy(p, j).start()
+    for n in range(3):
+        block_copy(n).start()
     for p in range(PIECES):
-        gather_end(0, p)
+        hand_wait(p, 0)
+    if local:
+        product((row // 2) * (rounds // chunk - 1), 1, tuple(range(PIECES)), True)
+    bring(0)
+    rest(0)
+    pair_start(0)
+    first_sum(0)
+    advance(0, 0)
+    bring(1)
+    rest(1)
+    pair_start(1)
+    advance(1, 0)
+    first_sum(1)
+    advance(2, 0)
+    advance(0, 1)
+    advance(3, 0)
+    advance(1, 1)
+    gather_on(0, 0)
+    advance(2, 1)
+    gather_on(0, 1)
+    gather_on(1, 0)
+    gather_end(0, 0)
+    gather_end(1, 0)
+    advance(3, 1)
+    gather_end(0, 1)
     cov_all[...] = outer(0)
-    for p in range(PIECES):
-        gather_on(1, p)
-    for p in range(PIECES):
-        gather_end(1, p)
+    gather_on(1, 1)
+    gather_end(1, 1)
     cov_all[...] += outer(1)
 
     rows = pl.ds(pl.multiple_of(col * share % 128, share), share)
@@ -214,6 +331,13 @@
 
     for j in range(1, n_row):
         cov_copy(j).wait_send()
+    for n in range(3):
+        block_copy(n).wait_send()
+    for j in range(1, band):
+        cross_copy(PIECES - 1, j).wait_send()
+    for p in range(PIECES):
+        for j in range(band):
+            hand_copy(p, j).wait_send()
     for p in range(PIECES):
         for panel in range(2):
             pair_copy(panel, p).wait_send()
@@ -237,24 +361,32 @@
                     gather_copy(g, p, dz).wait_send()
 
 
-def chain(n_row, n_col, pre, cross, gown, gpair, prior):
-    tiles, tile, sites = pre.shape
+def chain(n_row, n_col, left, prev, cross, inverses, coupling, prior):
+    tiles, tile, rounds, _ = left.shape
+    sites = prev.shape[2]
     half, n_z, owners, band = tiles // 2, n_col // 2, n_col // n_row, n_row // 2
     per = half // owners
     width = sites // 2 // PIECES
     share = prior.shape[0]
+    local = band == 2 and rounds % 16 == 0 and rounds >= 32
+    chunk = 16 if local else rounds
     dma = pltpu.SemaphoreType.DMA
     vm = pl.BlockSpec(memory_space=pltpu.VMEM)
+    hbm = pl.BlockSpec(memory_space=pl.ANY)
     return pl.pallas_call(
-        functools.partial(chain_kernel, n_row, n_col, tiles * tile * n_row),
+        functools.partial(chain_kernel, n_row, n_col, chunk, local, tiles * tile * n_row),
         out_shape=(
             jax.ShapeDtypeStruct((tiles, tile, sites), BF16),
             jax.ShapeDtypeStruct((share, sites), F32),
         ),
-        in_specs=[vm] * 5,
+        in_specs=[hbm, hbm] + [vm] * 4,
         out_specs=(vm, vm),
         scratch_shapes=[
-            pltpu.VMEM((PIECES, half, tile, width), F32),
+            pltpu.VMEM((tiles, tile, sites), F32),
+            pltpu.VMEM((PIECES, rounds, tile, 2 * width), BF16),
+            pltpu.VMEM((2, tile, chunk, tile), BF16),
+            pltpu.VMEM(inverses.shape, BF16),
+            pltpu.VMEM(coupling.shape, BF16),
             pltpu.VMEM((PIECES, half, tile, width), F32),
             pltpu.VMEM((4, PIECES, owners, per, tile, width), BF16),
             pltpu.VMEM((4, PIECES, n_z - 1, per, tile, width), BF16),
@@ -272,23 +404,21 @@
             dma((2, PIECES, n_z - 1)), dma((2, PIECES, owners)),
             dma((2, PIECES, owners)), dma((2, PIECES, owners)),
             dma((n_row - 1,)), dma((n_row - 1,)),
+            dma((PIECES,)), dma((2,)),
+            dma((PIECES, max(band - 1, 1))), dma((PIECES, max(band - 1, 1))),
+            dma((PIECES, band)), dma((PIECES, band)),
+            dma((3,)), dma((3,)),
         ],
         compiler_params=pltpu.CompilerParams(
-            collective_id=0, has_side_effects=True, vmem_limit_bytes=48 * 1024 * 1024),
-    )(pre, cross, gown, gpair, prior)
+            collective_id=0, has_side_effects=True, vmem_limit_bytes=60 * 1024 * 1024),
+    )(left, prev, cross, inverses, coupling, prior)
 
 
 def body(n_row, n_col, left_factor, prev_solution, cross, inverses, coupling, prior_cov):
     half, tile, cols, _ = coupling.shape
-    blocks = jnp.stack([inverses[0], coupling, inverses[1]]).reshape(3, half * tile, cols * tile)
-    mate = lax.ppermute(blocks, "col", [(c, c ^ 1) for c in range(n_col)])
-    pre = jnp.einsum(
-        "atbu,bum->atm",
-        left_factor,
-        lax.all_gather(prev_solution, "row", axis=0, tiled=True),
-        preferred_element_type=F32,
-    )
-    return chain(n_row, n_col, pre, cross, blocks, mate, prior_cov)
+    return chain(
+        n_row, n_col, left_factor, prev_solution, cross,
+        inverses.reshape(2, half * tile, cols * tile), coupling.reshape(half * tile, cols * tile), prior_cov)
 
 
 def solution(mesh):

time: 276 us -> 227 us (0.82); the launches traced: 276 us -> 224 us
  Pallas kernels: 118 us -> 215 us
  waiting for transfers between devices: 73.5 us -> 0 us
  matrix products: 56.9 us -> 0 us
  between operations: 14.1 us -> 0.66 us
  local copies, waits for them, and re-layouts: 12.2 us -> 8.93 us
    pallas_call x1, Pallas kernels: 118 us -> 215 us  [chain(): pl.pallas_call(functools.partial(chain_kernel, n_row, n_col, chunk, local...]
    all_gather x1 -> x0, waiting for transfers between devices: 72.8 us -> none  [body(): lax.all_gather(prev_solution, 'row', axis=0, tiled=True)]
    dot_general x1 -> x0, matrix products: 56.9 us -> none  [body(): jnp.einsum('atbu,bum->atm', left_factor, lax.all_gather(prev_solution, 'r...]
    another operation x4 -> x0, local copies, waits for them, and re-layouts: 4.19 us -> none  [body(): jnp.stack([inverses[0], coupling, inverses[1]])]
    slice x1 -> x0, local copies, waits for them, and re-layouts: 3.46 us -> none  [body(): inverses[1]]
    unnamed x10 -> x7, local copies, waits for them, and re-layouts: 4.55 us -> 6.34 us
  transfers between devices with their start and end apart: 2 -> 0, of which waited for: 1 -> 0; matrix products, arithmetic and copies ran while one was open for 24% -> 0% of each run, Pallas kernels for 0% -> 0%
where the time goes in v2:
time: 227 us; the launch traced here: 224 us
  Pallas kernels  215 us (95%)
  local copies, waits for them, and re-layouts  8.93 us (4%)
    pallas_call x1, Pallas kernels, chain(): pl.pallas_call(functools.partial(chain_kernel, n_row, n_col, chunk, local...  215 us
    unnamed x7, local copies, waits for them, and re-layouts  6.34 us

profile of v2, /device:TPU:27, one launch (start us, length us, event | category | flops | bytes accessed | tf_op | source)
XLA Modules:
  0.0 224.2 jit_solution(1646211575491284298)
XLA Ops:
  0.6 0.0 copy-start
  0.6 2.6 %copy.8 = bf16[128,8,2,256]{3,1,2,0:T(8,128)(2,1)} copy(bf16[128,8,2,256]{3,2,1,0:T(2,128)(2,1)} %bitcast.4) | data formatting | bytes 2097152
  3.2 0.0 copy-done
  3.2 2.6 %reshape.10.ginv_ref = bf16[2,1024,512]{2,1,0:T(8,128)(2,1)} reshape(bf16[2,4,256,2,256]{4,3,2,1,0:T(2,128)(2,1)S(1)} %copy-done) | data formatting | bytes 4194304 | tf_op jit(solution)/shard_map/reshape | solution.py:421
  5.8 214.6 %shard_map.77 = (bf16[8,256,512]{2,1,0:T(8,128)(2,1)}, f32[64,512]{1,0:T(8,128)}) custom-call(bf16[8,256,48,256]{3,2,1,0:T(8,128)(2,1)} %left_ref.1, bf16[12,256,512]{2,1,0:T(8,128)(2,1)} %prev_ref.1, bf16[8,256,512]{2,1,0:T(8,128)(2,1)} %cross_ref.1, bf16[2,1024,512]{2,1,0:T(8,128)(2,1)} %reshape.10.ginv_ref, bf16[1024,512]{1,0:T(8,128)(2,1)} %bitcast.3, ...), custom_call_target="tpu_custom_call" | custom-call | tf_op jit(solution)/shard_map/pallas_call | solution.py:376
  220.4 0.0 copy-start.1
  220.4 3.1 %copy.11 = bf16[8,256,512]{2,1,0:T(8,128)(2,1)} copy(bf16[8,256,512]{2,1,0:T(8,128)(2,1)} %get-tuple-element.4) | data formatting | bytes 4194304
  223.5 0.0 copy-done.1
  223.5 0.7 copy.12
Async XLA Ops:
  0.6 2.6 %copy-start = (bf16[2,4,256,2,256]{4,3,2,1,0:T(2,128)(2,1)S(1)}, bf16[2,4,256,2,256]{4,3,2,1,0:T(2,128)(2,1)}, u32[]{:S(2)}) copy-start(bf16[2,4,256,2,256]{4,3,2,1,0:T(2,128)(2,1)} %param.9) | copy-start | bytes 6291460
  220.4 3.1 %copy-start.1 = (f32[64,512]{1,0:T(8,128)S(1)}, f32[64,512]{1,0:T(8,128)}, u32[]{:S(2)}) copy-start(f32[64,512]{1,0:T(8,128)} %get-tuple-element.5) | copy-start | bytes 393220

commit v3 on v2

--- a/solution.py
+++ b/solution.py
@@ -15,11 +15,11 @@
 def chain_kernel(
     n_row, n_col, chunk, local, total_rows,
     left_ref, prev_ref, cross_ref, ginv_ref, gmid_ref, prior_ref,
-    out_ref, cov_ref,
-    pre_ref, solved_rows, left_buf, pinv, pmid, part, stage, land, rhs, sol, pair_out, pair_in, cov_out, cov_in, cov_all,
+    out_ref, cov_ref, flat_ref,
+    pre_ref, solved_rows, left_buf, flat_buf, pinv, pmid, part, stage, land, rhs, sol, pair_out, pair_in, cov_out, cov_in, cov_all,
     s_pair, r_pair, s_red, r_red, s_x, r_x, s_core, r_core,
     s_gat, r_gat, s_fwd, r_fwd, s_cov, r_cov,
-    l_own, l_left, s_vx, r_vx, s_vc, r_vc, s_g, r_g,
+    l_own, l_left, l_flat, s_vx, r_vx, s_vc, r_vc, s_g, r_g,
 ):
     tiles, tile, sites = pre_ref.shape
     half = tiles // 2
@@ -213,36 +213,104 @@
         dst = pmid if n == 1 else pinv.at[n // 2]
         return remote(src, dst, s_g.at[n], r_g.at[n], row, mate_col)
 
-    def product(first, chunks, pieces, fresh):
-        steps = tiles * chunks
-
-        def fetch(s, slot):
-            at = pl.multiple_of((first + s % chunks) * chunk, chunk)
-            return pltpu.make_async_copy(left_ref.at[s // chunks, :, pl.ds(at, chunk), :], left_buf.at[slot], l_left.at[slot])
-
-        fetch(0, 0).start()
-
-        def step(s, carry):
-            slot = s % 2
-
-            @pl.when(s + 1 < steps)
-            def _():
-                fetch(s + 1, 1 - slot).start()
-
-            fetch(s, slot).wait()
-            at = (first + s % chunks) * chunk
-            block = left_buf[slot].reshape(tile, chunk * tile)
-            for p in pieces:
-                values = solved_rows[p, pl.ds(at, chunk)].reshape(chunk * tile, wide)
-                got = jnp.dot(block, values, preferred_element_type=F32)
-                where = (s // chunks, slice(None), pl.ds(p * wide, wide))
-                if fresh:
-                    pre_ref[where] = got
-                else:
-                    pre_ref[where] += got
+    depth = chunk * tile
+    chunks = rounds // chunk
+    first = 1 - row // 2 if local else 0
+    blocks = (chunks - 1 if local else chunks) * tiles
+
+    def values(p, c):
+        return solved_rows[p, pl.ds(c * chunk, chunk)].reshape(depth, wide)
+
+    def add(p, a, c, block, fresh):
+        count = block.shape[0] // tile
+        got = jnp.dot(block, values(p, c), preferred_element_type=F32).reshape(count, tile, wide)
+        where = (pl.ds(a, count), slice(None), pl.ds(p * wide, wide))
+        if fresh:
+            pre_ref[where] = got
+        else:
+            pre_ref[where] += got
+
+    def fetch(a, c, slot):
+        at = pl.multiple_of(c * chunk, chunk)
+        return pltpu.make_async_copy(left_ref.at[a, :, pl.ds(at, chunk), :], left_buf.at[slot], l_left.at[slot])
+
+    def local_product():
+        c = (row // 2) * (chunks - 1)
+        fetch(0, c, 0).start()
+
+        def step(a, carry):
+            slot = a % 2
+
+            @pl.when(a + 1 < tiles)
+            def _():
+                fetch(a + 1, c, 1 - slot).start()
+
+            fetch(a, c, slot).wait()
+            block = left_buf[slot].reshape(tile, depth)
+            for p in range(PIECES):
+                add(p, a, c, block, True)
             return carry
 
-        lax.fori_loop(0, steps, step, 0)
+        lax.fori_loop(0, tiles, step, 0)
+
+    def save(s, slot):
+        return pltpu.make_async_copy(flat_buf.at[slot, 0], flat_ref.at[s], l_flat.at[slot])
+
+    def rearrange(low, high, p):
+        count = high - low
+
+        def get(n, slot):
+            s = low + n
+            return fetch(s % tiles, first + s // tiles, slot)
+
+        get(0, 0).start()
+
+        def step(n, carry):
+            slot = n % 2
+            s = low + n
+
+            @pl.when(n + 1 < count)
+            def _():
+                get(n + 1, 1 - slot).start()
+
+            get(n, slot).wait()
+
+            @pl.when(n >= 2)
+            def _():
+                save(s - 2, slot).wait()
+
+            block = left_buf[slot].reshape(tile, depth)
+            flat_buf[slot, 0] = block
+            save(s, slot).start()
+            if p is not None:
+                add(p, s % tiles, first + s // tiles, block, not local)
+            return carry
+
+        lax.fori_loop(0, count, step, 0)
+        save(high - 2, (count - 2) % 2).wait()
+        save(high - 1, (count - 1) % 2).wait()
+
+    def replay(low, high, p):
+        count = (high - low) // 2
+
+        def get(n, slot):
+            return pltpu.make_async_copy(flat_ref.at[pl.ds(low + 2 * n, 2)], flat_buf.at[slot], l_flat.at[slot])
+
+        get(0, 0).start()
+
+        def step(n, carry):
+            slot = n % 2
+
+            @pl.when(n + 1 < count)
+            def _():
+                get(n + 1, 1 - slot).start()
+
+            get(n, slot).wait()
+            s = low + 2 * n
+            add(p, s % tiles, first + s // tiles, flat_buf[slot].reshape(2 * tile, depth), not local)
+            return carry
+
+        lax.fori_loop(0, count, step, 0)
 
     def bring(p):
         for j in range(1, band):
@@ -256,13 +324,6 @@
         for j in range(1, band):
             hand_wait(p, j)
 
-    def rest(p):
-        if local:
-            product((1 - row // 2), rounds // chunk - 1, (p,), False)
-        else:
-            for n in range(rounds // chunk):
-                product(n, 1, (p,), n == 0)
-
     def first_sum(p):
         pair_copy(0, p).wait_recv()
         for a in range(half):
@@ -285,15 +346,19 @@
         block_copy(n).start()
     for p in range(PIECES):
         hand_wait(p, 0)
+    middle = blocks // 2
     if local:
-        product((row // 2) * (rounds // chunk - 1), 1, tuple(range(PIECES)), True)
+        local_product()
+    rearrange(0, middle, None)
     bring(0)
-    rest(0)
+    rearrange(middle, blocks, 0)
+    replay(0, middle, 0)
     pair_start(0)
     first_sum(0)
+    bring(1)
+    replay(0, middle, 1)
     advance(0, 0)
-    bring(1)
-    rest(1)
+    replay(middle, blocks, 1)
     pair_start(1)
     advance(1, 0)
     first_sum(1)
@@ -370,6 +435,7 @@
     share = prior.shape[0]
     local = band == 2 and rounds % 16 == 0 and rounds >= 32
     chunk = 16 if local else rounds
+    blocks = (rounds // chunk - (1 if local else 0)) * tiles
     dma = pltpu.SemaphoreType.DMA
     vm = pl.BlockSpec(memory_space=pltpu.VMEM)
     hbm = pl.BlockSpec(memory_space=pl.ANY)
@@ -378,13 +444,15 @@
         out_shape=(
             jax.ShapeDtypeStruct((tiles, tile, sites), BF16),
             jax.ShapeDtypeStruct((share, sites), F32),
+            jax.ShapeDtypeStruct((blocks, tile, chunk * tile), BF16),
         ),
         in_specs=[hbm, hbm] + [vm] * 4,
-        out_specs=(vm, vm),
+        out_specs=(vm, vm, hbm),
         scratch_shapes=[
             pltpu.VMEM((tiles, tile, sites), F32),
             pltpu.VMEM((PIECES, rounds, tile, 2 * width), BF16),
             pltpu.VMEM((2, tile, chunk, tile), BF16),
+            pltpu.VMEM((2, 2, tile, chunk * tile), BF16),
             pltpu.VMEM(inverses.shape, BF16),
             pltpu.VMEM(coupling.shape, BF16),
             pltpu.VMEM((PIECES, half, tile, width), F32),
@@ -404,14 +472,14 @@
             dma((2, PIECES, n_z - 1)), dma((2, PIECES, owners)),
             dma((2, PIECES, owners)), dma((2, PIECES, owners)),
             dma((n_row - 1,)), dma((n_row - 1,)),
-            dma((PIECES,)), dma((2,)),
+            dma((PIECES,)), dma((2,)), dma((2,)),
             dma((PIECES, max(band - 1, 1))), dma((PIECES, max(band - 1, 1))),
             dma((PIECES, band)), dma((PIECES, band)),
             dma((3,)), dma((3,)),
         ],
         compiler_params=pltpu.CompilerParams(
             collective_id=0, has_side_effects=True, vmem_limit_bytes=60 * 1024 * 1024),
-    )(left, prev, cross, inverses, coupling, prior)
+    )(left, prev, cross, inverses, coupling, prior)[:2]
 
 
 def body(n_row, n_col, left_factor, prev_solution, cross, inverses, coupling, prior_cov):

time: 227 us -> 216 us (0.952); the launches traced: 224 us -> 216 us
  Pallas kernels: 215 us -> 206 us
    pallas_call x1, Pallas kernels: 215 us -> 206 us  [chain(): pl.pallas_call(functools.partial(chain_kernel, n_row, n_col, chunk, local...]
where the time goes in v3:
time: 216 us
  Pallas kernels  206 us (95%)
  local copies, waits for them, and re-layouts  8.91 us (4%)
    pallas_call x1, Pallas kernels, chain(): pl.pallas_call(functools.partial(chain_kernel, n_row, n_col, chunk, local...  206 us
    unnamed x7, local copies, waits for them, and re-layouts  6.32 us

profile of v3, /device:TPU:27, one launch (start us, length us, event | category | flops | bytes accessed | tf_op | source)
XLA Modules:
  0.0 215.7 jit_solution(11747609521680626722)
XLA Ops:
  0.6 0.0 copy-start
  0.6 2.6 %copy.8 = bf16[128,8,2,256]{3,1,2,0:T(8,128)(2,1)} copy(bf16[128,8,2,256]{3,2,1,0:T(2,128)(2,1)} %bitcast.4) | data formatting | bytes 2097152
  3.2 0.0 copy-done
  3.2 2.6 %reshape.10.ginv_ref = bf16[2,1024,512]{2,1,0:T(8,128)(2,1)} reshape(bf16[2,4,256,2,256]{4,3,2,1,0:T(2,128)(2,1)S(1)} %copy-done) | data formatting | bytes 4194304 | tf_op jit(solution)/shard_map/reshape | solution.py:489
  5.8 206.2 %shard_map.77 = (bf16[8,256,512]{2,1,0:T(8,128)(2,1)}, f32[64,512]{1,0:T(8,128)}, bf16[16,256,4096]{2,1,0:T(8,128)(2,1)}) custom-call(bf16[8,256,48,256]{3,2,1,0:T(8,128)(2,1)} %left_ref.1, bf16[12,256,512]{2,1,0:T(8,128)(2,1)} %prev_ref.1, bf16[8,256,512]{2,1,0:T(8,128)(2,1)} %cross_ref.1, bf16[2,1024,512]{2,1,0:T(8,128)(2,1)} %reshape.10.ginv_ref, ...), custom_call_target="tpu_custom_call" | custom-call | tf_op jit(solution)/shard_map/pallas_call | solution.py:442
  212.0 0.0 copy-start.1
  212.0 3.1 %copy.11 = bf16[8,256,512]{2,1,0:T(8,128)(2,1)} copy(bf16[8,256,512]{2,1,0:T(8,128)(2,1)} %get-tuple-element.8) | data formatting | bytes 4194304
  215.1 0.0 copy-done.1
  215.1 0.7 copy.12
Async XLA Ops:
  0.6 2.6 %copy-start = (bf16[2,4,256,2,256]{4,3,2,1,0:T(2,128)(2,1)S(1)}, bf16[2,4,256,2,256]{4,3,2,1,0:T(2,128)(2,1)}, u32[]{:S(2)}) copy-start(bf16[2,4,256,2,256]{4,3,2,1,0:T(2,128)(2,1)} %param.9) | copy-start | bytes 6291460
  212.0 3.1 %copy-start.1 = (f32[64,512]{1,0:T(8,128)S(1)}, f32[64,512]{1,0:T(8,128)}, u32[]{:S(2)}) copy-start(f32[64,512]{1,0:T(8,128)} %get-tuple-element.9) | copy-start | bytes 393220
